TPU v7x, 256 devices: a whole 4x4x8 slice. The times are simulated.
256 devices in a mesh: dp: 16 (over z, core), expert: 16 (over y, x).
Axes of the slice: x: 4, y: 4, z: 8, core: 2. Of those that a mesh axis runs over, the one named last changes fastest.
Arguments:
- grad: float32 [16, 2048, 1408], P('expert', 'dp'), may hold values from -700 to 700
- expert_ids: int32 [16], replicated, may hold values from 0 to 15, each once
Outputs:
- update: bfloat16 [16, 2048, 1408], P('expert', 'dp')
Inputs may be any that keep to these rules, and one draw needn't show every extreme that they name: `expert_ids`: each of the 16 numbers appears once.
All inputs are finite; a program needn't handle non-finite values.
Results may differ from a plain program's by a relative error of at most 0.0065.
Values may be sent and summed in bfloat16 or wider, within the bound.
A program may use at most 64 MiB of HBM per device.

v0:
```python
import math

import jax
import jax.numpy as jnp
from jax import lax
from jax.sharding import PartitionSpec as P

D = 2048
F = 1408
ITERS = 2


coef_a = 3.4445
coef_b = -4.775
coef_c = 2.0315
gram_eps = 1e-07


def body(grad, expert_ids):
    dp_count = lax.axis_size("dp")
    team_count = lax.axis_size("expert")
    group_index = lax.axis_index("expert")
    per_group, block_rows, width = grad.shape
    quarter = block_rows // team_count
    total_slots = per_group * team_count
    owned = total_slots // dp_count
    width_part = width // team_count
    start_rows = grad.astype(jnp.bfloat16)
    spread = lax.all_to_all(
        start_rows.reshape(per_group, team_count, quarter, width),
        "expert",
        split_axis=1,
        concat_axis=0,
        tiled=True,
    )
    spread = spread.reshape(owned, dp_count, quarter, width)
    incoming = lax.all_to_all(spread, "dp", split_axis=1, concat_axis=1, tiled=True)
    team_rows = incoming.reshape(owned, dp_count * quarter, width)
    column_start = group_index * width_part
    current = team_rows
    mixed = current.astype(jnp.float32)
    for iteration in range(ITERS):
        partial_value = jnp.einsum(
            "snf,sng->sfg", current, current, preferred_element_type=jnp.float32
        )
        gram_part = lax.psum_scatter(partial_value, "expert", scatter_dimension=2, tiled=True)
        if iteration == 0:
            squares = lax.psum(jnp.sum(gram_part * gram_part, axis=(1, 2)), "expert")
            norm_value = jnp.sqrt(squares) + gram_eps
            inverse = 1.0 / norm_value
            row_factor = 1.0 / jnp.sqrt(norm_value)
        else:
            inverse = jnp.ones((owned,), jnp.float32)
            row_factor = jnp.ones((owned,), jnp.float32)
        scaled_part = (gram_part * inverse[:, None, None]).astype(jnp.bfloat16)
        gram = lax.all_gather(scaled_part, "expert", axis=2, tiled=True)
        gram_cols = lax.dynamic_slice_in_dim(gram, column_start, width_part, 2)
        cube_part = jnp.einsum("sfg,sgh->sfh", gram, gram_cols, preferred_element_type=jnp.float32)
        poly_part = (coef_b * gram_cols.astype(jnp.float32) + coef_c * cube_part).astype(
            jnp.bfloat16
        )
        poly = lax.all_gather(poly_part, "expert", axis=2, tiled=True)
        product = jnp.einsum("snf,sfg->sng", current, poly, preferred_element_type=jnp.float32)
        mixed = row_factor[:, None, None] * (coef_a * current.astype(jnp.float32) + product)
        if iteration < ITERS - 1:
            current = mixed.astype(jnp.bfloat16)
    update_rows = (math.sqrt(max(D, F)) * mixed).astype(jnp.bfloat16)
    outgoing_back = update_rows.reshape(owned, dp_count, quarter, width)
    returned = lax.all_to_all(outgoing_back, "dp", split_axis=1, concat_axis=1, tiled=True)
    returned = returned.reshape(total_slots, quarter, width)
    pick_back = (expert_ids[None, :] == jnp.arange(total_slots, dtype=jnp.int32)[:, None]).astype(
        jnp.bfloat16
    )
    by_expert = jnp.einsum(
        "es,skf->ekf", pick_back, returned, preferred_element_type=jnp.float32
    ).astype(jnp.bfloat16)
    final_rows = lax.all_to_all(
        by_expert.reshape(team_count, per_group, quarter, width),
        "expert",
        split_axis=0,
        concat_axis=2,
        tiled=True,
    )
    return final_rows.reshape(per_group, block_rows, width)


def solution(mesh):
    return jax.shard_map(
        body,
        mesh=mesh,
        in_specs=(P("expert", "dp", None), P()),
        out_specs=P("expert", "dp", None),
        check_vma=False,
    )
```

profile of v0, /device:TPU:1, one launch (start us, length us, event | category | flops | bytes accessed | tf_op | source)
XLA Modules:
  0.0 1908.2 jit_solution(6138005018739666993)
XLA Ops:
  6.5 1.1 convert_bitcast_fusion
  7.7 16.2 all_to_all.28
  23.9 23.9 %all_to_all.29 = bf16[1,16,8,1408]{3,2,0,1:T(8,128)(2,1)S(1)} all-to-all(bf16[1,16,8,1408]{3,2,0,1:T(8,128)(2,1)S(1)} %all_to_all.28), channel_id=1, replica_groups=mesh['dp'=16,'expert'=16] {'dp'}, dimensions={1} | all-to-all | bytes 720896 | tf_op jit(solution)/shard_map/all_to_all | solution.py:37
  47.9 4.4 convolution_bitcast_fusion.1
  52.3 21.4 %copy.23 = f32[1,1408,1408]{1,0,2:T(1,128)} copy(f32[1,1408,1408]{2,1,0:T(8,128)} %convolution_bitcast_fusion.1) | data formatting | bytes 15859712 | tf_op jit(solution)/shard_map/snf,sng->sfg/dot_general | solution.py:43
  75.5 138.5 %all-reduce.5.cloned.1.call-done = f32[1,1408,1408]{1,0,2:T(1,128)} async-done(((f32[1,1408,1408]{1,0,2:T(1,128)}), f32[1,1408,1408]{1,0,2:T(1,128)}) %all-reduce.5.cloned.1.call-update) | async-done | bytes 7929872
  214.0 2.7 multiply_reduce_fusion
  216.7 32.0 %psum.7 = f32[1]{0:T(128)} all-reduce(f32[1]{0:T(128)} %bitcast.6), channel_id=1, replica_groups=mesh['dp'=16,'expert'=16] {'expert'}, use_global_device_ids=true, to_apply=%region_2.0 | all-reduce | flops 1 | bytes 8 | tf_op jit(solution)/shard_map/psum | solution.py:48
  249.4 0.7 fusion.57
  250.2 59.7 %all-gather.5.cloned.1.call-done = bf16[1,1408,1408]{1,2,0:T(8,128)(2,1)} async-done(((bf16[1,1408,88]{1,2,0:T(8,128)(2,1)}), bf16[1,1408,1408]{1,2,0:T(8,128)(2,1)}) %all-gather.5.cloned.1.call-update) | async-done | bytes 3964944 | tf_op jit(solution)/shard_map/all_gather | solution.py:56
  310.0 3.7 fusion.50
  313.8 55.3 %all-gather.7.cloned.1.call-done = bf16[1,1408,1408]{1,2,0:T(8,128)(2,1)} async-done(((bf16[1,1408,88]{1,2,0:T(8,128)(2,1)}), bf16[1,1408,1408]{1,2,0:T(8,128)(2,1)}) %all-gather.7.cloned.1.call-update) | async-done | bytes 3964944 | tf_op jit(solution)/shard_map/all_gather | solution.py:62
  369.1 3.4 fusion.29
  372.5 4.4 convolution_bitcast_fusion
  376.9 21.4 %copy.25 = f32[1,1408,1408]{1,0,2:T(1,128)} copy(f32[1,1408,1408]{2,1,0:T(8,128)} %convolution_bitcast_fusion) | data formatting | bytes 15859712 | tf_op jit(solution)/shard_map/snf,sng->sfg/dot_general | solution.py:43
  398.3 1342.8 %all-reduce.6 = bf16[1,1408,1408]{1,0,2:T(2,128)(2,1)} all-reduce(f32[1,1408,1408]{1,0,2:T(1,128)} %copy.25), channel_id=3, replica_groups=mesh['dp'=16,'expert'=16] {'expert'}, use_global_device_ids=true, to_apply=%region_3.0.clone | all-reduce | flops 1982464 | bytes 11894784
  1741.1 1.5 dynamic-slice_convert_fusion
  1743.4 58.3 %all-gather.9.cloned.1.call-done = bf16[1,1408,1408]{1,2,0:T(8,128)(2,1)} async-done(((bf16[1,1408,88]{1,2,0:T(8,128)(2,1)}), bf16[1,1408,1408]{1,2,0:T(8,128)(2,1)}) %all-gather.9.cloned.1.call-update) | async-done | bytes 3964944 | tf_op jit(solution)/shard_map/all_gather | solution.py:56
  1801.7 3.7 fusion.47
  1805.4 55.4 %all-gather.11.cloned.1.call-done = bf16[1,1408,1408]{1,2,0:T(8,128)(2,1)} async-done(((bf16[1,1408,88]{1,2,0:T(8,128)(2,1)}), bf16[1,1408,1408]{1,2,0:T(8,128)(2,1)}) %all-gather.11.cloned.1.call-update) | async-done | bytes 3964944 | tf_op jit(solution)/shard_map/all_gather | solution.py:62
  1860.8 3.4 fusion.53
  1864.2 21.5 %all_to_all.30 = bf16[1,16,8,1408]{3,2,0,1:T(8,128)(2,1)S(1)} all-to-all(bf16[1,16,8,1408]{3,2,0,1:T(8,128)(2,1)S(1)} %fusion.53), channel_id=1, replica_groups=mesh['dp'=16,'expert'=16] {'dp'}, dimensions={1} | all-to-all | bytes 720896 | tf_op jit(solution)/shard_map/all_to_all | solution.py:69
  1886.0 14.9 all_to_all.31
  1900.9 0.7 copy.45
  (18 shorter events, 2.5 us)
Async XLA Ops:
  6.5 207.5 %all-reduce.5.cloned.1.call-start = ((), (), s32[]{:S(2)}) async-start(), calls=%async_computation.8 | async-start | bytes 15859712
  73.6 0.7 copy-start.1
  73.6 236.3 %all-gather.5.cloned.1.call-start = ((), (), s32[]{:S(2)}) async-start(), calls=%async_computation.4 | async-start | bytes 4212736 | tf_op jit(solution)/shard_map/all_gather | solution.py:56
  250.2 118.9 %all-gather.7.cloned.1.call-start = ((), (), s32[]{:S(2)}) async-start(), calls=%async_computation.5 | async-start | bytes 4212736 | tf_op jit(solution)/shard_map/all_gather | solution.py:62
  313.7 1488.0 %all-gather.9.cloned.1.call-start = ((), (), s32[]{:S(2)}) async-start(), calls=%async_computation.6 | async-start | bytes 4212736 | tf_op jit(solution)/shard_map/all_gather | solution.py:56
  1743.4 117.5 %all-gather.11.cloned.1.call-start = ((), (), s32[]{:S(2)}) async-start(), calls=%async_computation.7 | async-start | bytes 4212736 | tf_op jit(solution)/shard_map/all_gather | solution.py:62
  1805.4 80.3 %copy-start = (s32[16]{0:T(128)S(1)}, s32[16]{0:T(128)}, u32[]{:S(2)}) copy-start(s32[16]{0:T(128)} %param.3) | copy-start | bytes 196
Sparse Core Ops, SparseCore 0:
  73.8 140.2 all-reduce.4
  250.3 59.6 all-gather.4
  313.8 55.2 all-gather.6
  1743.5 58.1 all-gather.8
  1805.5 55.2 all-gather.10
where the time goes:
time: 1910 us
  blocking collectives  1450 us (76%)
  waiting for transfers between devices  367 us (19%)
  local copies, waits for them, and re-layouts  47 us (2%)
  matrix products  23.2 us (1%)
    unnamed x1, blocking collectives  1340 us
    unnamed x6, waiting for transfers between devices  139 us
    all_gather x2, waiting for transfers between devices, body(): gram = lax.all_gather(scaled_part, 'expert', axis=2, tiled=True)  118 us
    all_gather x2, waiting for transfers between devices, body(): poly = lax.all_gather(poly_part, 'expert', axis=2, tiled=True)  111 us
    dot_general x2, local copies, waits for them, and re-layouts, body(): jnp.einsum('snf,sng->sfg', current, current, preferred_element_type=jnp.f...  42.7 us
  transfers between devices with their start and end apart: 5, of which 5 were waited for; matrix products, arithmetic and copies ran while one was open for 0% of the time, Pallas kernels for 0%

commit v1 on v0

v1 whole, which is shorter than its diff:
```python
import math

import jax
import jax.numpy as jnp
from jax import lax
from jax.experimental import pallas as pl
from jax.experimental.pallas import tpu as pltpu
from jax.sharding import PartitionSpec as P

D = 2048
F = 1408
ROWS = 128
GROUP = 16
GROUPS = 8
TEAM = 16
RING = 8
STEPS = 8

coef_a = 3.4445
coef_b = -4.775
coef_c = 2.0315
gram_eps = 1e-07

MESH = pl.DeviceIdType.MESH
PANELS = [(i, min(256, F - i)) for i in range(0, F, 256)]


def kernel(
    grad_ref,
    ids_ref,
    out_ref,
    own,
    mid,
    stage,
    slots,
    turned,
    gram,
    amat,
    base,
    once,
    total,
    first,
    send1,
    recv1,
    send2,
    recv2,
    send_up,
    recv_up,
    send_down,
    recv_down,
    send_sib,
    recv_sib,
):
    dp = lax.axis_index("dp")
    me = lax.axis_index("expert")
    core = lax.rem(dp, 2)
    z = dp // 2
    sib = dp + 1 - 2 * core
    up = lax.rem(z + 1, RING) * 2 + core
    down = lax.rem(z + RING - 1, RING) * 2 + core

    barrier = pltpu.get_barrier_semaphore()
    for k in range(1, TEAM):
        pl.semaphore_signal(
            barrier, inc=1, device_id=(dp, lax.rem(me + k, TEAM)), device_id_type=MESH
        )
    for other in (sib, up, down):
        pl.semaphore_signal(barrier, inc=1, device_id=(other, me), device_id_type=MESH)
    own[...] = grad_ref[...].reshape(GROUPS, GROUP, F).astype(jnp.bfloat16)
    pl.semaphore_wait(barrier, TEAM + 2)

    def copy1(g):
        return pltpu.make_async_remote_copy(
            src_ref=own.at[g],
            dst_ref=mid.at[me],
            send_sem=send1.at[g],
            recv_sem=recv1.at[me],
            device_id=(dp, 2 * g + core),
            device_id_type=MESH,
        )

    def arrive1(s):
        return pltpu.make_async_remote_copy(
            src_ref=own.at[0],
            dst_ref=mid.at[s],
            send_sem=send1.at[0],
            recv_sem=recv1.at[s],
            device_id=(dp, s),
            device_id_type=MESH,
        )

    def copy2(e, g):
        return pltpu.make_async_remote_copy(
            src_ref=stage.at[e],
            dst_ref=slots.at[0, g],
            send_sem=send2.at[e],
            recv_sem=recv2.at[g],
            device_id=(dp, e),
            device_id_type=MESH,
        )

    def arrive2(g):
        return pltpu.make_async_remote_copy(
            src_ref=stage.at[0],
            dst_ref=slots.at[0, g],
            send_sem=send2.at[0],
            recv_sem=recv2.at[g],
            device_id=(dp, 2 * g + core),
            device_id_type=MESH,
        )

    my_group = me // 2
    relay = lax.rem(me, 2) == core

    @pl.loop(0, GROUPS)
    def _(g):
        @pl.when(2 * g + core != me)
        def _():
            copy1(g).start()

    @pl.when(relay)
    def _():
        mid[me] = own[my_group]

    gram[...] = jnp.zeros_like(gram)

    @pl.when(relay)
    def _():
        @pl.loop(0, TEAM)
        def _(s):
            @pl.when(s != me)
            def _():
                arrive1(s).wait_recv()

        @pl.loop(0, TEAM)
        def _(k):
            e = lax.rem(me + k, TEAM)
            slot = jnp.int32(0)
            for j in range(TEAM):
                slot = jnp.where(ids_ref[j] == e, j, slot)
            stage[e] = mid[slot]

            @pl.when(e == me)
            def _():
                slots[0, my_group] = stage[e]

            @pl.when(e != me)
            def _():
                copy2(e, my_group).start()

    @pl.loop(0, GROUPS)
    def _(g):
        @pl.when(2 * g + core != me)
        def _():
            arrive2(g).wait_recv()

    half = GROUPS // 2
    lower, upper = pl.ds(0, half), pl.ds(half, half)

    def copy_up(src, part, t):
        return pltpu.make_async_remote_copy(
            src_ref=slots.at[src, part],
            dst_ref=slots.at[t, lower],
            send_sem=send_up.at[t],
            recv_sem=recv_up.at[t],
            device_id=(up, me),
            device_id_type=MESH,
        )

    def copy_down(src, part, t):
        return pltpu.make_async_remote_copy(
            src_ref=slots.at[src, part],
            dst_ref=slots.at[t, upper],
            send_sem=send_down.at[t],
            recv_sem=recv_down.at[t],
            device_id=(down, me),
            device_id_type=MESH,
        )

    def copy_sib(t):
        return pltpu.make_async_remote_copy(
            src_ref=slots.at[t, pl.ds(0, GROUPS)],
            dst_ref=slots.at[t, pl.ds(GROUPS, GROUPS)],
            send_sem=send_sib.at[t],
            recv_sem=recv_sib.at[t],
            device_id=(sib, me),
            device_id_type=MESH,
        )

    copy_up(0, lower, 1).start()
    copy_down(0, upper, 1).start()
    copy_up(0, upper, 2).start()
    copy_down(0, lower, 2).start()

    @pl.loop(0, STEPS)
    def _(t):
        @pl.when(t > 0)
        def _():
            copy_up(t, lower, t).wait_recv()
            copy_down(t, upper, t).wait_recv()

            @pl.when(t + 2 < STEPS)
            def _():
                copy_up(t, lower, t + 2).start()
                copy_down(t, upper, t + 2).start()

        copy_sib(t).start()
        copy_sib(t).wait_recv()
        rows = slots[t].reshape(2 * ROWS, F)
        turned[...] = rows.T
        for start, size in PANELS:
            gram[:, start : start + size] += jnp.dot(
                turned[...],
                slots[t, :, :, start : start + size].reshape(2 * ROWS, size),
                preferred_element_type=jnp.float32,
            )

    def square(i, acc):
        g = gram[pl.ds(pl.multiple_of(i * 128, 128), 128), :]
        return acc + jnp.sum((g * g).reshape(16, 8, F), axis=0)

    squares = lax.fori_loop(0, F // 128, square, jnp.zeros((8, F), jnp.float32))
    norm = jnp.sqrt(jnp.sum(squares, keepdims=True).reshape(1, 1)) + gram_eps
    inverse = 1.0 / norm
    factor = 1.0 / jnp.sqrt(norm)

    @pl.loop(0, F // 128)
    def _(i):
        part = pl.ds(pl.multiple_of(i * 128, 128), 128)
        amat[part, :] = (gram[part, :] * inverse).astype(jnp.bfloat16)

    def times(dst, src):
        x = src[...].astype(jnp.bfloat16)
        for start, size in PANELS:
            dst[:, start : start + size] = jnp.dot(
                x, amat[:, start : start + size], preferred_element_type=jnp.float32
            )

    def poly():
        times(once, base)
        base[...] = coef_a * base[...] + coef_b * once[...]
        x = once[...].astype(jnp.bfloat16)
        for start, size in PANELS:
            base[:, start : start + size] += coef_c * jnp.dot(
                x, amat[:, start : start + size], preferred_element_type=jnp.float32
            )

    base[...] = slots[0, 0:GROUPS].reshape(ROWS, F).astype(jnp.float32)
    poly()
    first[...] = (factor * base[...]).astype(jnp.bfloat16)
    base[...] = first[...].astype(jnp.float32)
    total[...] = coef_a * base[...]

    @pl.loop(0, 2)
    def _(it):
        poly()
        times(once, base)
        base[...] = once[...]
        poly()
        total[...] += jnp.where(it == 0, coef_b, coef_c) * base[...]

    out_ref[...] = (math.sqrt(max(D, F)) * total[...]).astype(jnp.bfloat16)

    @pl.loop(0, GROUPS)
    def _(g):
        @pl.when(2 * g + core != me)
        def _():
            copy1(g).wait_send()

    @pl.when(relay)
    def _():
        @pl.loop(0, TEAM)
        def _(e):
            @pl.when(e != me)
            def _():
                copy2(e, my_group).wait_send()

    @pl.loop(0, STEPS)
    def _(t):
        copy_sib(t).wait_send()

        @pl.when(t > 0)
        def _():
            copy_up(t, lower, t).wait_send()
            copy_down(t, upper, t).wait_send()


def body(grad, expert_ids):
    dma = pltpu.SemaphoreType.DMA
    bf16, f32 = jnp.bfloat16, jnp.float32
    out = pl.pallas_call(
        kernel,
        out_shape=jax.ShapeDtypeStruct((ROWS, F), bf16),
        in_specs=[
            pl.BlockSpec(memory_space=pltpu.VMEM),
            pl.BlockSpec(memory_space=pltpu.SMEM),
        ],
        out_specs=pl.BlockSpec(memory_space=pltpu.VMEM),
        scratch_shapes=[
            pltpu.VMEM((GROUPS, GROUP, F), bf16),
            pltpu.VMEM((TEAM, GROUP, F), bf16),
            pltpu.VMEM((TEAM, GROUP, F), bf16),
            pltpu.VMEM((STEPS, 2 * GROUPS, GROUP, F), bf16),
            pltpu.VMEM((F, 2 * ROWS), bf16),
            pltpu.VMEM((F, F), f32),
            pltpu.VMEM((F, F), bf16),
            pltpu.VMEM((ROWS, F), f32),
            pltpu.VMEM((ROWS, F), f32),
            pltpu.VMEM((ROWS, F), f32),
            pltpu.VMEM((ROWS, F), bf16),
            dma((GROUPS,)),
            dma((TEAM,)),
            dma((TEAM,)),
            dma((GROUPS,)),
            dma((STEPS,)),
            dma((STEPS,)),
            dma((STEPS,)),
            dma((STEPS,)),
            dma((STEPS,)),
            dma((STEPS,)),
        ],
        compiler_params=pltpu.CompilerParams(
            collective_id=0,
            has_side_effects=True,
            vmem_limit_bytes=48 * 1024 * 1024,
        ),
        cost_estimate=pl.CostEstimate(
            flops=2 * F * F * (D + 12 * ROWS), bytes_accessed=6 * ROWS * F, transcendentals=0
        ),
    )(grad.reshape(ROWS, F), expert_ids)
    return out.reshape(1, ROWS, F)


def solution(mesh):
    return jax.shard_map(
        body,
        mesh=mesh,
        in_specs=(P("expert", "dp", None), P()),
        out_specs=P("expert", "dp", None),
        check_vma=False,
    )
```

time: 1910 us -> 69.4 us (0.04)
  blocking collectives: 1450 us -> 0 us
  waiting for transfers between devices: 367 us -> 0 us
  Pallas kernels: 0 us -> 66.8 us
  local copies, waits for them, and re-layouts: 47 us -> 2.5 us
  matrix products: 23.2 us -> 0 us
    unnamed x1 -> x0, blocking collectives: 1340 us -> none
    all_gather x4 -> x0, waiting for transfers between devices: 229 us -> none  [the longest x2 118 us: body(): gram = lax.all_gather(scaled_part, 'expert', axis=2, tiled=True)]
    unnamed x6 -> x0, waiting for transfers between devices: 139 us -> none
    all_to_all x4 -> x0, blocking collectives: 76.5 us -> none  [the longest x1 23.9 us: body(): lax.all_to_all(spread, 'dp', split_axis=1, concat_axis=1, tiled=True)]
    pallas_call x0 -> x1, Pallas kernels: none -> 66.8 us  [body(): pl.pallas_call(kernel, out_shape=jax.ShapeDtypeStruct((ROWS, F), bf16), i...]
    dot_general x2 -> x0, local copies, waits for them, and re-layouts: 42.7 us -> none  [body(): jnp.einsum('snf,sng->sfg', current, current, preferred_element_type=jnp.f...]
    psum x1 -> x0, blocking collectives: 32 us -> none  [body(): squares = lax.psum(jnp.sum(gram_part * gram_part, axis=(1, 2)), 'expert')]
    dot_general x7 -> x0, matrix products: 23.2 us -> none  [the longest x2 8.81 us: body(): jnp.einsum('snf,sng->sfg', current, current, preferred_element_type=jnp.f...]
  transfers between devices with their start and end apart: 5 -> 0, of which waited for: 5 -> 0; matrix products, arithmetic and copies ran while one was open for 0% -> 0% of each run, Pallas kernels for 0% -> 0%
where the time goes in v1:
time: 69.4 us; the launch traced here: 69.3 us
  Pallas kernels  66.8 us (96%)
  local copies, waits for them, and re-layouts  2.5 us (4%)
    pallas_call x1, Pallas kernels, body(): pl.pallas_call(kernel, out_shape=jax.ShapeDtypeStruct((ROWS, F), bf16), i...  66.8 us
    unnamed x5, local copies, waits for them, and re-layouts  2.5 us

profile of v1, /device:TPU:1, one launch (start us, length us, event | category | flops | bytes accessed | tf_op | source)
XLA Modules:
  0.0 69.3 jit_solution(5140740484375525009)
XLA Ops:
  0.0 0.0 copy-start.1
  0.0 0.7 copy-done.1
  0.7 0.0 copy-start
  0.7 1.1 %copy-done = f32[1,128,1408]{2,1,0:T(8,128)S(1)} copy-done((f32[1,128,1408]{2,1,0:T(8,128)S(1)}, f32[1,128,1408]{2,1,0:T(8,128)}, u32[]{:S(2)}) %copy-start) | copy-done | bytes 720920
  1.8 66.8 %shard_map.28 = bf16[128,1408]{1,0:T(8,128)(2,1)S(1)} custom-call(f32[128,1408]{1,0:T(8,128)S(1)} %bitcast.3, s32[16]{0:T(128)S(1)} %copy-done.1), custom_call_target="tpu_custom_call" | custom-call | flops 14210301952 | bytes 1081344 | tf_op jit(solution)/shard_map/pallas_call | solution.py:291
  68.5 0.7 %copy.4 = bf16[1,128,1408]{2,1,0:T(8,128)(2,1)} copy(bf16[1,128,1408]{2,1,0:T(8,128)(2,1)S(1)} %bitcast.2) | data formatting | bytes 720896
Async XLA Ops:
  0.0 0.7 copy-start.1
  0.7 1.1 %copy-start = (f32[1,128,1408]{2,1,0:T(8,128)S(1)}, f32[1,128,1408]{2,1,0:T(8,128)}, u32[]{:S(2)}) copy-start(f32[1,128,1408]{2,1,0:T(8,128)} %param.2) | copy-start | bytes 2162692

commit v2 on v1

v2 whole, which is shorter than its diff:
```python
import math

import jax
import jax.numpy as jnp
from jax import lax
from jax.experimental import pallas as pl
from jax.experimental.pallas import tpu as pltpu
from jax.sharding import PartitionSpec as P

D = 2048
F = 1408
ROWS = 128
GROUP = 16
GROUPS = 8
TEAM = 16
RING = 8
STEPS = 8

coef_a = 3.4445
coef_b = -4.775
coef_c = 2.0315
gram_eps = 1e-07

MESH = pl.DeviceIdType.MESH
SPLIT = [(0, 640), (640, 768)]
PANELS = [(i, min(256, F - i)) for i in range(0, F, 256)]


def kernel(
    grad_ref,
    ids_ref,
    out_ref,
    raw,
    ids,
    holder,
    own,
    mid,
    stage,
    slots,
    turned,
    gram,
    amat,
    base,
    total,
    left,
    right,
    load_raw,
    load_ids,
    send1,
    recv1,
    send2,
    recv2,
    send_up,
    recv_up,
    send_down,
    recv_down,
    send_sib,
    recv_sib,
):
    dp = lax.axis_index("dp")
    me = lax.axis_index("expert")
    core = lax.rem(dp, 2)
    z = dp // 2
    sib = dp + 1 - 2 * core
    up = lax.rem(z + 1, RING) * 2 + core
    down = lax.rem(z + RING - 1, RING) * 2 + core

    fetch_raw = pltpu.make_async_copy(grad_ref, raw, load_raw)
    fetch_ids = pltpu.make_async_copy(ids_ref, ids, load_ids)
    fetch_raw.start()
    fetch_ids.start()
    barrier = pltpu.get_barrier_semaphore()

    @pl.loop(1, TEAM)
    def _(k):
        pl.semaphore_signal(
            barrier, inc=1, device_id=(dp, lax.rem(me + k, TEAM)), device_id_type=MESH
        )

    for other in (sib, up, down):
        pl.semaphore_signal(barrier, inc=1, device_id=(other, me), device_id_type=MESH)
    fetch_raw.wait()
    own[...] = raw[...].reshape(GROUPS, GROUP, F).astype(jnp.bfloat16)
    fetch_ids.wait()

    @pl.loop(0, TEAM)
    def _(e):
        slot = jnp.int32(0)
        for j in range(TEAM):
            slot = jnp.where(ids[j] == e, j, slot)
        holder[e] = slot

    pl.semaphore_wait(barrier, TEAM + 2)

    def relay_of(wave, row, side):
        return 4 * row + 2 * side + lax.rem(row + wave + core, 2)

    my_x, my_y = lax.rem(me, 4), me // 4
    my_group = 4 * lax.rem(my_x + my_y + core, 2) + my_y
    my_side = my_x // 2

    def piece(side):
        return pl.ds(*SPLIT[side])

    def copy1(wave, row, side):
        g = 4 * wave + row
        return pltpu.make_async_remote_copy(
            src_ref=own.at[g, :, piece(side)],
            dst_ref=mid.at[me, :, piece(side)],
            send_sem=send1.at[2 * g + side],
            recv_sem=recv1.at[me],
            device_id=(dp, relay_of(wave, row, side)),
            device_id_type=MESH,
        )

    def arrive1(s, side):
        return pltpu.make_async_remote_copy(
            src_ref=own.at[0, :, piece(side)],
            dst_ref=mid.at[s, :, piece(side)],
            send_sem=send1.at[0],
            recv_sem=recv1.at[s],
            device_id=(dp, s),
            device_id_type=MESH,
        )

    def copy2(e, side):
        return pltpu.make_async_remote_copy(
            src_ref=stage.at[e, :, piece(side)],
            dst_ref=slots.at[0, my_group, :, piece(side)],
            send_sem=send2.at[e],
            recv_sem=recv2.at[2 * my_group + side],
            device_id=(dp, e),
            device_id_type=MESH,
        )

    def arrive2(wave, row, side):
        g = 4 * wave + row
        return pltpu.make_async_remote_copy(
            src_ref=stage.at[0, :, piece(side)],
            dst_ref=slots.at[0, g, :, piece(side)],
            send_sem=send2.at[0],
            recv_sem=recv2.at[2 * g + side],
            device_id=(dp, relay_of(wave, row, side)),
            device_id_type=MESH,
        )

    for wave in range(2):

        @pl.loop(0, 4)
        def _(k):
            row = lax.rem(k + me, 4)
            for side in range(2):

                @pl.when(relay_of(wave, row, side) != me)
                def _():
                    copy1(wave, row, side).start()

    for side in range(2):

        @pl.when(my_side == side)
        def _():
            mid[me, :, piece(side)] = own[my_group, :, piece(side)]

    gram[...] = jnp.zeros_like(gram)

    for side in range(2):

        @pl.when(my_side == side)
        def _():
            @pl.loop(0, TEAM)
            def _(s):
                @pl.when(s != me)
                def _():
                    arrive1(s, side).wait_recv()

            @pl.loop(0, TEAM)
            def _(k):
                e = lax.rem(me + k, TEAM)
                stage[e, :, piece(side)] = mid[holder[e], :, piece(side)]

                @pl.when(e == me)
                def _():
                    slots[0, my_group, :, piece(side)] = stage[e, :, piece(side)]

                @pl.when(e != me)
                def _():
                    copy2(e, side).start()

    def part(first_group, count):
        return pl.ds(first_group, count)

    half = GROUPS // 2
    lower, upper = part(0, half), part(half, half)

    def copy_up(src, src_part, t, dst_part, sem):
        return pltpu.make_async_remote_copy(
            src_ref=slots.at[src, src_part],
            dst_ref=slots.at[t, dst_part],
            send_sem=send_up.at[sem],
            recv_sem=recv_up.at[sem],
            device_id=(up, me),
            device_id_type=MESH,
        )

    def copy_down(src, src_part, t, dst_part, sem):
        return pltpu.make_async_remote_copy(
            src_ref=slots.at[src, src_part],
            dst_ref=slots.at[t, dst_part],
            send_sem=send_down.at[sem],
            recv_sem=recv_down.at[sem],
            device_id=(down, me),
            device_id_type=MESH,
        )

    def copy_sib(t):
        return pltpu.make_async_remote_copy(
            src_ref=slots.at[t, part(0, GROUPS)],
            dst_ref=slots.at[t, part(GROUPS, GROUPS)],
            send_sem=send_sib.at[t],
            recv_sem=recv_sib.at[t],
            device_id=(sib, me),
            device_id_type=MESH,
        )

    def down_piece(src, t, p):
        rows = part(half + 2 * p, 2)
        return copy_down(src, rows, t, rows, STEPS - 2 + 2 * (t - (STEPS - 2)) + p)

    for wave in range(2):

        @pl.loop(0, 4)
        def _(row):
            for side in range(2):

                @pl.when(relay_of(wave, row, side) != me)
                def _():
                    arrive2(wave, row, side).wait_recv()

        sent = part(4 * wave, 4)
        copy_up(0, sent, wave + 1, lower, wave + 1).start()
        copy_down(0, sent, wave + 1, upper, wave + 1).start()

    def turn(t):
        turned[...] = slots[t].reshape(2 * ROWS, F).T

    def columns(t, start, size):
        return slots[t, :, :, start : start + size].reshape(2 * ROWS, size)

    def meet(t):
        copy_sib(t).start()
        copy_sib(t).wait_recv()
        turn(t)

    @pl.loop(0, STEPS - 1)
    def _(t):
        @pl.when(t == STEPS - 2)
        def _():
            for p in range(2):
                down_piece(4, 6, p).wait_recv()
                down_piece(6, 7, p).start()
            copy_up(4, lower, 6, lower, 6).wait_recv()

        @pl.when((t > 0) & (t < STEPS - 2))
        def _():
            copy_up(t, lower, t, lower, t).wait_recv()
            copy_up(t, lower, t + 2, lower, t + 2).start()
            copy_down(t, upper, t, upper, t).wait_recv()

            @pl.when(t < STEPS - 4)
            def _():
                copy_down(t, upper, t + 2, upper, t + 2).start()

            @pl.when(t == STEPS - 4)
            def _():
                for p in range(2):
                    down_piece(4, 6, p).start()

        meet(t)
        for start, size in PANELS:
            end = start + size
            gram[0:end, start:end] += jnp.dot(
                turned[0:end, :], columns(t, start, size), preferred_element_type=jnp.float32
            )

    last = STEPS - 1
    copy_up(5, lower, last, lower, last).wait_recv()
    for p in range(2):
        down_piece(6, last, p).wait_recv()
    meet(last)
    squares = jnp.zeros((8, 128), jnp.float32)
    for start, size in PANELS:
        end = start + size
        panel = columns(last, start, size)
        for row, count in PANELS:
            if row > start:
                break
            rows = slice(row, row + count)
            g = gram[rows, start:end] + jnp.dot(
                turned[rows, :], panel, preferred_element_type=jnp.float32
            )
            amat[rows, start:end] = g.astype(jnp.bfloat16)
            folded = jnp.sum((g * g).reshape(count // 8, 8, size), axis=0)
            for lane in range(0, size, 128):
                lanes = folded[:, lane : lane + 128]
                squares = squares + (lanes if row == start else 2.0 * lanes)
        if start:
            amat[start:end, 0:start] = amat[0:start, start:end].T
    norm = jnp.sqrt(jnp.sum(squares, keepdims=True)) + gram_eps
    inverse = 1.0 / norm
    factor = 1.0 / jnp.sqrt(norm)

    def product(src, finish):
        for start, size in PANELS:
            cols = slice(start, start + size)
            finish(
                cols,
                inverse
                * jnp.dot(src[...], amat[:, cols], preferred_element_type=jnp.float32),
            )

    def poly(src, spare, finish):
        def linear(cols, u):
            base[:, cols] = coef_a * base[:, cols] + coef_b * u
            spare[:, cols] = u.astype(jnp.bfloat16)

        def quadratic(cols, u):
            finish(cols, base[:, cols] + coef_c * u)

        product(src, linear)
        product(spare, quadratic)

    def keep(dst):
        def finish(cols, value):
            base[:, cols] = value
            dst[:, cols] = value.astype(jnp.bfloat16)

        return finish

    def first(cols, value):
        y = (factor * value).astype(jnp.bfloat16)
        left[:, cols] = y
        base[:, cols] = y.astype(jnp.float32)
        total[:, cols] = coef_a * y.astype(jnp.float32)

    def second(cols, value):
        keep(right)(cols, value)
        total[:, cols] += coef_b * value

    def third(cols, value):
        result = total[:, cols] + coef_c * value
        out_ref[:, cols] = (math.sqrt(max(D, F)) * result).astype(jnp.bfloat16)

    left[...] = slots[0, 0:GROUPS].reshape(ROWS, F)
    base[...] = left[...].astype(jnp.float32)
    poly(left, right, first)
    poly(left, right, keep(left))
    product(left, keep(right))
    poly(right, left, second)
    poly(right, left, keep(right))
    product(right, keep(left))
    poly(left, right, third)

    for wave in range(2):

        @pl.loop(0, 4)
        def _(row):
            for side in range(2):

                @pl.when(relay_of(wave, row, side) != me)
                def _():
                    copy1(wave, row, side).wait_send()

    for side in range(2):

        @pl.when(my_side == side)
        def _():
            @pl.loop(0, TEAM)
            def _(e):
                @pl.when(e != me)
                def _():
                    copy2(e, side).wait_send()

    @pl.loop(0, STEPS)
    def _(t):
        copy_sib(t).wait_send()

        @pl.when(t > 0)
        def _():
            copy_up(t, lower, t, lower, t).wait_send()

            @pl.when(t < STEPS - 2)
            def _():
                copy_down(t, upper, t, upper, t).wait_send()

    for p in range(2):
        down_piece(4, 6, p).wait_send()
        down_piece(6, 7, p).wait_send()


def body(grad, expert_ids):
    dma = pltpu.SemaphoreType.DMA
    bf16, f32 = jnp.bfloat16, jnp.float32
    out = pl.pallas_call(
        kernel,
        out_shape=jax.ShapeDtypeStruct((ROWS, F), bf16),
        in_specs=[pl.BlockSpec(memory_space=pl.ANY)] * 2,
        out_specs=pl.BlockSpec(memory_space=pltpu.VMEM),
        scratch_shapes=[
            pltpu.VMEM((ROWS, F), f32),
            pltpu.SMEM((TEAM,), jnp.int32),
            pltpu.SMEM((TEAM,), jnp.int32),
            pltpu.VMEM((GROUPS, GROUP, F), bf16),
            pltpu.VMEM((TEAM, GROUP, F), bf16),
            pltpu.VMEM((TEAM, GROUP, F), bf16),
            pltpu.VMEM((STEPS, 2 * GROUPS, GROUP, F), bf16),
            pltpu.VMEM((F, 2 * ROWS), bf16),
            pltpu.VMEM((F, F), f32),
            pltpu.VMEM((F, F), bf16),
            pltpu.VMEM((ROWS, F), f32),
            pltpu.VMEM((ROWS, F), f32),
            pltpu.VMEM((ROWS, F), bf16),
            pltpu.VMEM((ROWS, F), bf16),
            dma,
            dma,
            dma((2 * GROUPS,)),
            dma((TEAM,)),
            dma((TEAM,)),
            dma((2 * GROUPS,)),
            dma((STEPS,)),
            dma((STEPS,)),
            dma((STEPS + 2,)),
            dma((STEPS + 2,)),
            dma((STEPS,)),
            dma((STEPS,)),
        ],
        compiler_params=pltpu.CompilerParams(
            collective_id=0,
            has_side_effects=True,
            vmem_limit_bytes=55800000,
        ),
        cost_estimate=pl.CostEstimate(
            flops=2 * F * F * (D + 12 * ROWS), bytes_accessed=6 * ROWS * F, transcendentals=0
        ),
    )(grad.reshape(ROWS, F), expert_ids)
    return out.reshape(1, ROWS, F)


def solution(mesh):
    return jax.shard_map(
        body,
        mesh=mesh,
        in_specs=(P("expert", "dp", None), P()),
        out_specs=P("expert", "dp", None),
        check_vma=False,
    )
```

time: 69.4 us -> 63.5 us (0.915)
  Pallas kernels: 66.8 us -> 62 us
  local copies, waits for them, and re-layouts: 2.5 us -> 1.39 us
    pallas_call x1, Pallas kernels: 66.8 us -> 62 us  [body(): pl.pallas_call(kernel, out_shape=jax.ShapeDtypeStruct((ROWS, F), bf16), i...]
    unnamed x5 -> x3, local copies, waits for them, and re-layouts: 2.5 us -> 1.39 us
where the time goes in v2:
time: 63.5 us; the launch traced here: 63.4 us
  Pallas kernels  62 us (98%)
  local copies, waits for them, and re-layouts  1.39 us (2%)
    pallas_call x1, Pallas kernels, body(): pl.pallas_call(kernel, out_shape=jax.ShapeDtypeStruct((ROWS, F), bf16), i...  62 us
    unnamed x3, local copies, waits for them, and re-layouts  1.39 us

profile of v2, /device:TPU:1, one launch (start us, length us, event | category | flops | bytes accessed | tf_op | source)
XLA Modules:
  0.0 63.4 jit_solution(9654896957500982127)
XLA Ops:
  0.0 0.0 copy-start
  0.0 0.7 %copy-done = s32[16]{0:T(128)S(1)} copy-done((s32[16]{0:T(128)S(1)}, s32[16]{0:T(128)}, u32[]{:S(2)}) %copy-start) | copy-done | bytes 88
  0.7 62.0 %shard_map.28 = bf16[128,1408]{1,0:T(8,128)(2,1)S(1)} custom-call(f32[128,1408]{1,0:T(8,128)} %bitcast.3, s32[16]{0:T(128)S(1)} %copy-done), custom_call_target="tpu_custom_call" | custom-call | flops 14210301952 | bytes 1081344 | tf_op jit(solution)/shard_map/pallas_call | solution.py:403
  62.6 0.7 %copy.4 = bf16[1,128,1408]{2,1,0:T(8,128)(2,1)} copy(bf16[1,128,1408]{2,1,0:T(8,128)(2,1)S(1)} %bitcast.2) | data formatting | bytes 720896
Async XLA Ops:
  0.0 0.7 %copy-start = (s32[16]{0:T(128)S(1)}, s32[16]{0:T(128)}, u32[]{:S(2)}) copy-start(s32[16]{0:T(128)} %ids_ref.1) | copy-start | bytes 196

commit v3 on v2

--- a/solution.py
+++ b/solution.py
@@ -247,20 +247,24 @@
         return slots[t, :, :, start : start + size].reshape(2 * ROWS, size)
 
     def meet(t):
-        copy_sib(t).start()
         copy_sib(t).wait_recv()
         turn(t)
 
+    copy_sib(0).start()
+
     @pl.loop(0, STEPS - 1)
-    def _(t):
+    def _(k):
+        t = k + 1
+
         @pl.when(t == STEPS - 2)
         def _():
             for p in range(2):
                 down_piece(4, 6, p).wait_recv()
                 down_piece(6, 7, p).start()
             copy_up(4, lower, 6, lower, 6).wait_recv()
-
-        @pl.when((t > 0) & (t < STEPS - 2))
+            copy_sib(t).start()
+
+        @pl.when(t < STEPS - 2)
         def _():
             copy_up(t, lower, t, lower, t).wait_recv()
             copy_up(t, lower, t + 2, lower, t + 2).start()
@@ -275,17 +279,20 @@
                 for p in range(2):
                     down_piece(4, 6, p).start()
 
-        meet(t)
+            copy_sib(t).start()
+
+        meet(k)
         for start, size in PANELS:
             end = start + size
             gram[0:end, start:end] += jnp.dot(
-                turned[0:end, :], columns(t, start, size), preferred_element_type=jnp.float32
+                turned[0:end, :], columns(k, start, size), preferred_element_type=jnp.float32
             )
 
     last = STEPS - 1
     copy_up(5, lower, last, lower, last).wait_recv()
     for p in range(2):
         down_piece(6, last, p).wait_recv()
+    copy_sib(last).start()
     meet(last)
     squares = jnp.zeros((8, 128), jnp.float32)
     for start, size in PANELS:

time: 63.5 us -> 62.9 us (level)
  Pallas kernels: 62 us -> 61.3 us
where the time goes in v3:
time: 62.9 us; the launch traced here: 62.7 us
  Pallas kernels  61.3 us (97%)
  local copies, waits for them, and re-layouts  1.39 us (2%)
    pallas_call x1, Pallas kernels, body(): pl.pallas_call(kernel, out_shape=jax.ShapeDtypeStruct((ROWS, F), bf16), i...  61.3 us
    unnamed x3, local copies, waits for them, and re-layouts  1.39 us

profile of v3, /device:TPU:1, one launch (start us, length us, event | category | flops | bytes accessed | tf_op | source)
XLA Modules:
  0.0 62.7 jit_solution(7004299096605856269)
XLA Ops:
  0.0 0.0 copy-start
  0.0 0.7 %copy-done = s32[16]{0:T(128)S(1)} copy-done((s32[16]{0:T(128)S(1)}, s32[16]{0:T(128)}, u32[]{:S(2)}) %copy-start) | copy-done | bytes 88
  0.7 61.3 %shard_map.28 = bf16[128,1408]{1,0:T(8,128)(2,1)S(1)} custom-call(f32[128,1408]{1,0:T(8,128)} %bitcast.3, s32[16]{0:T(128)S(1)} %copy-done), custom_call_target="tpu_custom_call" | custom-call | flops 14210301952 | bytes 1081344 | tf_op jit(solution)/shard_map/pallas_call | solution.py:410
  62.0 0.7 %copy.4 = bf16[1,128,1408]{2,1,0:T(8,128)(2,1)} copy(bf16[1,128,1408]{2,1,0:T(8,128)(2,1)S(1)} %bitcast.2) | data formatting | bytes 720896
Async XLA Ops:
  0.0 0.7 %copy-start = (s32[16]{0:T(128)S(1)}, s32[16]{0:T(128)}, u32[]{:S(2)}) copy-start(s32[16]{0:T(128)} %ids_ref.1) | copy-start | bytes 196

commit v4 on v3

--- a/solution.py
+++ b/solution.py
@@ -23,6 +23,7 @@
 
 MESH = pl.DeviceIdType.MESH
 SPLIT = [(0, 640), (640, 768)]
+WIDE = [(0, F)]
 PANELS = [(i, min(256, F - i)) for i in range(0, F, 256)]
 
 
@@ -317,7 +318,7 @@
     factor = 1.0 / jnp.sqrt(norm)
 
     def product(src, finish):
-        for start, size in PANELS:
+        for start, size in WIDE:
             cols = slice(start, start + size)
             finish(
                 cols,

time: 62.9 us -> 62.9 us (level)
  no operation moved by 1% of the time
where the time goes in v4:
time: 62.9 us; the launch traced here: 62.8 us
  Pallas kernels  61.4 us (98%)
  local copies, waits for them, and re-layouts  1.39 us (2%)
    pallas_call x1, Pallas kernels, body(): pl.pallas_call(kernel, out_shape=jax.ShapeDtypeStruct((ROWS, F), bf16), i...  61.4 us
    unnamed x3, local copies, waits for them, and re-layouts  1.39 us

profile of v4, /device:TPU:1, one launch (start us, length us, event | category | flops | bytes accessed | tf_op | source)
XLA Modules:
  0.0 62.8 jit_solution(8341325375670957989)
XLA Ops:
  0.0 0.0 copy-start
  0.0 0.7 %copy-done = s32[16]{0:T(128)S(1)} copy-done((s32[16]{0:T(128)S(1)}, s32[16]{0:T(128)}, u32[]{:S(2)}) %copy-start) | copy-done | bytes 88
  0.7 61.4 %shard_map.28 = bf16[128,1408]{1,0:T(8,128)(2,1)S(1)} custom-call(f32[128,1408]{1,0:T(8,128)} %bitcast.3, s32[16]{0:T(128)S(1)} %copy-done), custom_call_target="tpu_custom_call" | custom-call | flops 14210301952 | bytes 1081344 | tf_op jit(solution)/shard_map/pallas_call | solution.py:411
  62.0 0.7 %copy.4 = bf16[1,128,1408]{2,1,0:T(8,128)(2,1)} copy(bf16[1,128,1408]{2,1,0:T(8,128)(2,1)S(1)} %bitcast.2) | data formatting | bytes 720896
Async XLA Ops:
  0.0 0.7 %copy-start = (s32[16]{0:T(128)S(1)}, s32[16]{0:T(128)}, u32[]{:S(2)}) copy-start(s32[16]{0:T(128)} %ids_ref.1) | copy-start | bytes 196

commit v5 on v4

--- a/solution.py
+++ b/solution.py
@@ -82,6 +82,77 @@
         pl.semaphore_signal(barrier, inc=1, device_id=(other, me), device_id_type=MESH)
     fetch_raw.wait()
     own[...] = raw[...].reshape(GROUPS, GROUP, F).astype(jnp.bfloat16)
+    pl.semaphore_wait(barrier, TEAM + 2)
+
+    def relay_of(wave, row, side):
+        return 4 * row + 2 * side + lax.rem(row + wave + core, 2)
+
+    my_x, my_y = lax.rem(me, 4), me // 4
+    my_group = 4 * lax.rem(my_x + my_y + core, 2) + my_y
+    my_side = my_x // 2
+
+    def piece(side):
+        return pl.ds(*SPLIT[side])
+
+    def copy1(wave, row, side):
+        g = 4 * wave + row
+        return pltpu.make_async_remote_copy(
+            src_ref=own.at[g, :, piece(side)],
+            dst_ref=mid.at[me, :, piece(side)],
+            send_sem=send1.at[2 * g + side],
+            recv_sem=recv1.at[me],
+            device_id=(dp, relay_of(wave, row, side)),
+            device_id_type=MESH,
+        )
+
+    def arrive1(s, side):
+        return pltpu.make_async_remote_copy(
+            src_ref=own.at[0, :, piece(side)],
+            dst_ref=mid.at[s, :, piece(side)],
+            send_sem=send1.at[0],
+            recv_sem=recv1.at[s],
+            device_id=(dp, s),
+            device_id_type=MESH,
+        )
+
+    def copy2(e, side):
+        return pltpu.make_async_remote_copy(
+            src_ref=stage.at[e, :, piece(side)],
+            dst_ref=slots.at[0, my_group, :, piece(side)],
+            send_sem=send2.at[e],
+            recv_sem=recv2.at[2 * my_group + side],
+            device_id=(dp, e),
+            device_id_type=MESH,
+        )
+
+    def arrive2(wave, row, side):
+        g = 4 * wave + row
+        return pltpu.make_async_remote_copy(
+            src_ref=stage.at[0, :, piece(side)],
+            dst_ref=slots.at[0, g, :, piece(side)],
+            send_sem=send2.at[0],
+            recv_sem=recv2.at[2 * g + side],
+            device_id=(dp, relay_of(wave, row, side)),
+            device_id_type=MESH,
+        )
+
+    for wave in range(2):
+
+        @pl.loop(0, 4)
+        def _(k):
+            row = lax.rem(k + me, 4)
+            for side in range(2):
+
+                @pl.when(relay_of(wave, row, side) != me)
+                def _():
+                    copy1(wave, row, side).start()
+
+    for side in range(2):
+
+        @pl.when(my_side == side)
+        def _():
+            mid[me, :, piece(side)] = own[my_group, :, piece(side)]
+
     fetch_ids.wait()
 
     @pl.loop(0, TEAM)
@@ -91,79 +162,6 @@
             slot = jnp.where(ids[j] == e, j, slot)
         holder[e] = slot
 
-    pl.semaphore_wait(barrier, TEAM + 2)
-
-    def relay_of(wave, row, side):
-        return 4 * row + 2 * side + lax.rem(row + wave + core, 2)
-
-    my_x, my_y = lax.rem(me, 4), me // 4
-    my_group = 4 * lax.rem(my_x + my_y + core, 2) + my_y
-    my_side = my_x // 2
-
-    def piece(side):
-        return pl.ds(*SPLIT[side])
-
-    def copy1(wave, row, side):
-        g = 4 * wave + row
-        return pltpu.make_async_remote_copy(
-            src_ref=own.at[g, :, piece(side)],
-            dst_ref=mid.at[me, :, piece(side)],
-            send_sem=send1.at[2 * g + side],
-            recv_sem=recv1.at[me],
-            device_id=(dp, relay_of(wave, row, side)),
-            device_id_type=MESH,
-        )
-
-    def arrive1(s, side):
-        return pltpu.make_async_remote_copy(
-            src_ref=own.at[0, :, piece(side)],
-            dst_ref=mid.at[s, :, piece(side)],
-            send_sem=send1.at[0],
-            recv_sem=recv1.at[s],
-            device_id=(dp, s),
-            device_id_type=MESH,
-        )
-
-    def copy2(e, side):
-        return pltpu.make_async_remote_copy(
-            src_ref=stage.at[e, :, piece(side)],
-            dst_ref=slots.at[0, my_group, :, piece(side)],
-            send_sem=send2.at[e],
-            recv_sem=recv2.at[2 * my_group + side],
-            device_id=(dp, e),
-            device_id_type=MESH,
-        )
-
-    def arrive2(wave, row, side):
-        g = 4 * wave + row
-        return pltpu.make_async_remote_copy(
-            src_ref=stage.at[0, :, piece(side)],
-            dst_ref=slots.at[0, g, :, piece(side)],
-            send_sem=send2.at[0],
-            recv_sem=recv2.at[2 * g + side],
-            device_id=(dp, relay_of(wave, row, side)),
-            device_id_type=MESH,
-        )
-
-    for wave in range(2):
-
-        @pl.loop(0, 4)
-        def _(k):
-            row = lax.rem(k + me, 4)
-            for side in range(2):
-
-                @pl.when(relay_of(wave, row, side) != me)
-                def _():
-                    copy1(wave, row, side).start()
-
-    for side in range(2):
-
-        @pl.when(my_side == side)
-        def _():
-            mid[me, :, piece(side)] = own[my_group, :, piece(side)]
-
-    gram[...] = jnp.zeros_like(gram)
-
     for side in range(2):
 
         @pl.when(my_side == side)
@@ -227,6 +225,9 @@
         rows = part(half + 2 * p, 2)
         return copy_down(src, rows, t, rows, STEPS - 2 + 2 * (t - (STEPS - 2)) + p)
 
+    gram[...] = jnp.zeros_like(gram)
+    base[...] = jnp.zeros_like(base)
+
     for wave in range(2):
 
         @pl.loop(0, 4)
@@ -252,6 +253,13 @@
         turn(t)
 
     copy_sib(0).start()
+    left[...] = slots[0, 0:GROUPS].reshape(ROWS, F)
+
+    def apply(t):
+        inner = jnp.dot(left[...], turned[...], preferred_element_type=jnp.float32)
+        base[...] += jnp.dot(
+            inner.astype(jnp.bfloat16), columns(t, 0, F), preferred_element_type=jnp.float32
+        )
 
     @pl.loop(0, STEPS - 1)
     def _(k):
@@ -288,6 +296,7 @@
             gram[0:end, start:end] += jnp.dot(
                 turned[0:end, :], columns(k, start, size), preferred_element_type=jnp.float32
             )
+        apply(k)
 
     last = STEPS - 1
     copy_up(5, lower, last, lower, last).wait_recv()
@@ -295,6 +304,7 @@
         down_piece(6, last, p).wait_recv()
     copy_sib(last).start()
     meet(last)
+    apply(last)
     squares = jnp.zeros((8, 128), jnp.float32)
     for start, size in PANELS:
         end = start + size
@@ -326,16 +336,16 @@
                 * jnp.dot(src[...], amat[:, cols], preferred_element_type=jnp.float32),
             )
 
+    def linear(cols, x, u, spare):
+        base[:, cols] = coef_a * x + coef_b * u
+        spare[:, cols] = u.astype(jnp.bfloat16)
+
+    def quadratic(spare, finish):
+        product(spare, lambda cols, u: finish(cols, base[:, cols] + coef_c * u))
+
     def poly(src, spare, finish):
-        def linear(cols, u):
-            base[:, cols] = coef_a * base[:, cols] + coef_b * u
-            spare[:, cols] = u.astype(jnp.bfloat16)
-
-        def quadratic(cols, u):
-            finish(cols, base[:, cols] + coef_c * u)
-
-        product(src, linear)
-        product(spare, quadratic)
+        product(src, lambda cols, u: linear(cols, base[:, cols], u, spare))
+        quadratic(spare, finish)
 
     def keep(dst):
         def finish(cols, value):
@@ -358,9 +368,8 @@
         result = total[:, cols] + coef_c * value
         out_ref[:, cols] = (math.sqrt(max(D, F)) * result).astype(jnp.bfloat16)
 
-    left[...] = slots[0, 0:GROUPS].reshape(ROWS, F)
-    base[...] = left[...].astype(jnp.float32)
-    poly(left, right, first)
+    linear(slice(0, F), left[...].astype(jnp.float32), inverse * base[...], right)
+    quadratic(right, first)
     poly(left, right, keep(left))
     product(left, keep(right))
     poly(right, left, second)

time: 62.9 us -> 63.7 us (1.013)
  Pallas kernels: 61.4 us -> 62.2 us
    pallas_call x1, Pallas kernels: 61.4 us -> 62.2 us  [body(): pl.pallas_call(kernel, out_shape=jax.ShapeDtypeStruct((ROWS, F), bf16), i...]
where the time goes in v5:
time: 63.7 us; the launch traced here: 63.6 us
  Pallas kernels  62.2 us (98%)
  local copies, waits for them, and re-layouts  1.39 us (2%)
    pallas_call x1, Pallas kernels, body(): pl.pallas_call(kernel, out_shape=jax.ShapeDtypeStruct((ROWS, F), bf16), i...  62.2 us
    unnamed x3, local copies, waits for them, and re-layouts  1.39 us

profile of v5, /device:TPU:1, one launch (start us, length us, event | category | flops | bytes accessed | tf_op | source)
XLA Modules:
  0.0 63.6 jit_solution(14306859649419245380)
XLA Ops:
  0.0 0.0 copy-start
  0.0 0.7 %copy-done = s32[16]{0:T(128)S(1)} copy-done((s32[16]{0:T(128)S(1)}, s32[16]{0:T(128)}, u32[]{:S(2)}) %copy-start) | copy-done | bytes 88
  0.7 62.2 %shard_map.28 = bf16[128,1408]{1,0:T(8,128)(2,1)S(1)} custom-call(f32[128,1408]{1,0:T(8,128)} %bitcast.3, s32[16]{0:T(128)S(1)} %copy-done), custom_call_target="tpu_custom_call" | custom-call | flops 14210301952 | bytes 1081344 | tf_op jit(solution)/shard_map/pallas_call | solution.py:420
  62.8 0.7 %copy.4 = bf16[1,128,1408]{2,1,0:T(8,128)(2,1)} copy(bf16[1,128,1408]{2,1,0:T(8,128)(2,1)S(1)} %bitcast.2) | data formatting | bytes 720896
Async XLA Ops:
  0.0 0.7 %copy-start = (s32[16]{0:T(128)S(1)}, s32[16]{0:T(128)}, u32[]{:S(2)}) copy-start(s32[16]{0:T(128)} %ids_ref.1) | copy-start | bytes 196

commit v6 on v5

--- a/solution.py
+++ b/solution.py
@@ -292,9 +292,8 @@
 
         meet(k)
         for start, size in PANELS:
-            end = start + size
-            gram[0:end, start:end] += jnp.dot(
-                turned[0:end, :], columns(k, start, size), preferred_element_type=jnp.float32
+            gram[:, start : start + size] += jnp.dot(
+                turned[...], columns(k, start, size), preferred_element_type=jnp.float32
             )
         apply(k)
 
@@ -310,8 +309,6 @@
         end = start + size
         panel = columns(last, start, size)
         for row, count in PANELS:
-            if row > start:
-                break
             rows = slice(row, row + count)
             g = gram[rows, start:end] + jnp.dot(
                 turned[rows, :], panel, preferred_element_type=jnp.float32
@@ -319,10 +316,7 @@
             amat[rows, start:end] = g.astype(jnp.bfloat16)
             folded = jnp.sum((g * g).reshape(count // 8, 8, size), axis=0)
             for lane in range(0, size, 128):
-                lanes = folded[:, lane : lane + 128]
-                squares = squares + (lanes if row == start else 2.0 * lanes)
-        if start:
-            amat[start:end, 0:start] = amat[0:start, start:end].T
+                squares = squares + folded[:, lane : lane + 128]
     norm = jnp.sqrt(jnp.sum(squares, keepdims=True)) + gram_eps
     inverse = 1.0 / norm
     factor = 1.0 / jnp.sqrt(norm)

time: 63.7 us -> 65.3 us (1.025)
  Pallas kernels: 62.2 us -> 63.8 us
    pallas_call x1, Pallas kernels: 62.2 us -> 63.8 us  [body(): pl.pallas_call(kernel, out_shape=jax.ShapeDtypeStruct((ROWS, F), bf16), i...]
where the time goes in v6:
time: 65.3 us; the launch traced here: 65.2 us
  Pallas kernels  63.8 us (98%)
  local copies, waits for them, and re-layouts  1.39 us (2%)
    pallas_call x1, Pallas kernels, body(): pl.pallas_call(kernel, out_shape=jax.ShapeDtypeStruct((ROWS, F), bf16), i...  63.8 us
    unnamed x3, local copies, waits for them, and re-layouts  1.39 us

profile of v6, /device:TPU:1, one launch (start us, length us, event | category | flops | bytes accessed | tf_op | source)
XLA Modules:
  0.0 65.2 jit_solution(8530140737052376156)
XLA Ops:
  0.0 0.0 copy-start
  0.0 0.7 %copy-done = s32[16]{0:T(128)S(1)} copy-done((s32[16]{0:T(128)S(1)}, s32[16]{0:T(128)}, u32[]{:S(2)}) %copy-start) | copy-done | bytes 88
  0.7 63.8 %shard_map.28 = bf16[128,1408]{1,0:T(8,128)(2,1)S(1)} custom-call(f32[128,1408]{1,0:T(8,128)} %bitcast.3, s32[16]{0:T(128)S(1)} %copy-done), custom_call_target="tpu_custom_call" | custom-call | flops 14210301952 | bytes 1081344 | tf_op jit(solution)/shard_map/pallas_call | solution.py:414
  64.4 0.7 %copy.4 = bf16[1,128,1408]{2,1,0:T(8,128)(2,1)} copy(bf16[1,128,1408]{2,1,0:T(8,128)(2,1)S(1)} %bitcast.2) | data formatting | bytes 720896
Async XLA Ops:
  0.0 0.7 %copy-start = (s32[16]{0:T(128)S(1)}, s32[16]{0:T(128)}, u32[]{:S(2)}) copy-start(s32[16]{0:T(128)} %ids_ref.1) | copy-start | bytes 196

commit v7 on v5

--- a/solution.py
+++ b/solution.py
@@ -154,12 +154,11 @@
             mid[me, :, piece(side)] = own[my_group, :, piece(side)]
 
     fetch_ids.wait()
-
-    @pl.loop(0, TEAM)
-    def _(e):
+    values = [ids[j] for j in range(TEAM)]
+    for e in range(TEAM):
         slot = jnp.int32(0)
         for j in range(TEAM):
-            slot = jnp.where(ids[j] == e, j, slot)
+            slot = jnp.where(values[j] == e, j, slot)
         holder[e] = slot
 
     for side in range(2):
@@ -172,18 +171,14 @@
                 def _():
                     arrive1(s, side).wait_recv()
 
-            @pl.loop(0, TEAM)
+            for e in range(TEAM):
+                stage[e, :, piece(side)] = mid[holder[e], :, piece(side)]
+
+            @pl.loop(1, TEAM)
             def _(k):
-                e = lax.rem(me + k, TEAM)
-                stage[e, :, piece(side)] = mid[holder[e], :, piece(side)]
-
-                @pl.when(e == me)
-                def _():
-                    slots[0, my_group, :, piece(side)] = stage[e, :, piece(side)]
-
-                @pl.when(e != me)
-                def _():
-                    copy2(e, side).start()
+                copy2(lax.rem(me + k, TEAM), side).start()
+
+            slots[0, my_group, :, piece(side)] = stage[me, :, piece(side)]
 
     def part(first_group, count):
         return pl.ds(first_group, count)
@@ -225,9 +220,6 @@
         rows = part(half + 2 * p, 2)
         return copy_down(src, rows, t, rows, STEPS - 2 + 2 * (t - (STEPS - 2)) + p)
 
-    gram[...] = jnp.zeros_like(gram)
-    base[...] = jnp.zeros_like(base)
-
     for wave in range(2):
 
         @pl.loop(0, 4)
@@ -238,21 +230,29 @@
                 def _():
                     arrive2(wave, row, side).wait_recv()
 
+        if wave == 1:
+            copy_sib(0).start()
+            copy_up(0, lower, 1, lower, 1).wait_send()
+            copy_down(0, lower, 1, upper, 1).wait_send()
         sent = part(4 * wave, 4)
         copy_up(0, sent, wave + 1, lower, wave + 1).start()
         copy_down(0, sent, wave + 1, upper, wave + 1).start()
 
-    def turn(t):
-        turned[...] = slots[t].reshape(2 * ROWS, F).T
+    def turn(t, side):
+        turned[:, side * ROWS : (side + 1) * ROWS] = (
+            slots[t, side * GROUPS : (side + 1) * GROUPS].reshape(ROWS, F).T
+        )
 
     def columns(t, start, size):
         return slots[t, :, :, start : start + size].reshape(2 * ROWS, size)
 
     def meet(t):
+        turn(t, 0)
         copy_sib(t).wait_recv()
-        turn(t)
-
-    copy_sib(0).start()
+        turn(t, 1)
+
+    gram[...] = jnp.zeros_like(gram)
+    base[...] = jnp.zeros_like(base)
     left[...] = slots[0, 0:GROUPS].reshape(ROWS, F)
 
     def apply(t):
@@ -297,6 +297,39 @@
                 turned[0:end, :], columns(k, start, size), preferred_element_type=jnp.float32
             )
         apply(k)
+
+    for wave in range(2):
+
+        @pl.loop(0, 4)
+        def _(row):
+            for side in range(2):
+
+                @pl.when(relay_of(wave, row, side) != me)
+                def _():
+                    copy1(wave, row, side).wait_send()
+
+    for side in range(2):
+
+        @pl.when(my_side == side)
+        def _():
+            @pl.loop(1, TEAM)
+            def _(k):
+                copy2(lax.rem(me + k, TEAM), side).wait_send()
+
+    @pl.loop(2, STEPS - 1)
+    def _(t):
+        copy_up(t, lower, t, lower, t).wait_send()
+
+        @pl.when(t < STEPS - 2)
+        def _():
+            copy_down(t, upper, t, upper, t).wait_send()
+
+    @pl.loop(0, STEPS - 1)
+    def _(t):
+        copy_sib(t).wait_send()
+
+    for p in range(2):
+        down_piece(4, 6, p).wait_send()
 
     last = STEPS - 1
     copy_up(5, lower, last, lower, last).wait_recv()
@@ -377,41 +410,10 @@
     product(right, keep(left))
     poly(left, right, third)
 
-    for wave in range(2):
-
-        @pl.loop(0, 4)
-        def _(row):
-            for side in range(2):
-
-                @pl.when(relay_of(wave, row, side) != me)
-                def _():
-                    copy1(wave, row, side).wait_send()
-
-    for side in range(2):
-
-        @pl.when(my_side == side)
-        def _():
-            @pl.loop(0, TEAM)
-            def _(e):
-                @pl.when(e != me)
-                def _():
-                    copy2(e, side).wait_send()
-
-    @pl.loop(0, STEPS)
-    def _(t):
-        copy_sib(t).wait_send()
-
-        @pl.when(t > 0)
-        def _():
-            copy_up(t, lower, t, lower, t).wait_send()
-
-            @pl.when(t < STEPS - 2)
-            def _():
-                copy_down(t, upper, t, upper, t).wait_send()
-
-    for p in range(2):
-        down_piece(4, 6, p).wait_send()
-        down_piece(6, 7, p).wait_send()
+    down_piece(6, last, 0).wait_send()
+    down_piece(6, last, 1).wait_send()
+    copy_up(5, lower, last, lower, last).wait_send()
+    copy_sib(last).wait_send()
 
 
 def body(grad, expert_ids):

time: 63.7 us -> 64.5 us (1.013)
  Pallas kernels: 62.2 us -> 63 us
    pallas_call x1, Pallas kernels: 62.2 us -> 63 us  [body(): pl.pallas_call(kernel, out_shape=jax.ShapeDtypeStruct((ROWS, F), bf16), i...]
where the time goes in v7:
time: 64.5 us; the launch traced here: 64.4 us
  Pallas kernels  63 us (98%)
  local copies, waits for them, and re-layouts  1.39 us (2%)
    pallas_call x1, Pallas kernels, body(): pl.pallas_call(kernel, out_shape=jax.ShapeDtypeStruct((ROWS, F), bf16), i...  63 us
    unnamed x3, local copies, waits for them, and re-layouts  1.39 us

profile of v7, /device:TPU:1, one launch (start us, length us, event | category | flops | bytes accessed | tf_op | source)
XLA Modules:
  0.0 64.4 jit_solution(8833801171960496498)
XLA Ops:
  0.0 0.0 copy-start
  0.0 0.7 %copy-done = s32[16]{0:T(128)S(1)} copy-done((s32[16]{0:T(128)S(1)}, s32[16]{0:T(128)}, u32[]{:S(2)}) %copy-start) | copy-done | bytes 88
  0.7 63.0 %shard_map.28 = bf16[128,1408]{1,0:T(8,128)(2,1)S(1)} custom-call(f32[128,1408]{1,0:T(8,128)} %bitcast.3, s32[16]{0:T(128)S(1)} %copy-done), custom_call_target="tpu_custom_call" | custom-call | flops 14210301952 | bytes 1081344 | tf_op jit(solution)/shard_map/pallas_call | solution.py:422
  63.6 0.7 %copy.4 = bf16[1,128,1408]{2,1,0:T(8,128)(2,1)} copy(bf16[1,128,1408]{2,1,0:T(8,128)(2,1)S(1)} %bitcast.2) | data formatting | bytes 720896
Async XLA Ops:
  0.0 0.7 %copy-start = (s32[16]{0:T(128)S(1)}, s32[16]{0:T(128)}, u32[]{:S(2)}) copy-start(s32[16]{0:T(128)} %ids_ref.1) | copy-start | bytes 196

commit v8 on v7

--- a/solution.py
+++ b/solution.py
@@ -66,9 +66,13 @@
     up = lax.rem(z + 1, RING) * 2 + core
     down = lax.rem(z + RING - 1, RING) * 2 + core
 
-    fetch_raw = pltpu.make_async_copy(grad_ref, raw, load_raw)
+    def fetch_raw(q):
+        rows = pl.ds(32 * q, 32)
+        return pltpu.make_async_copy(grad_ref.at[rows], raw.at[rows], load_raw.at[q])
+
     fetch_ids = pltpu.make_async_copy(ids_ref, ids, load_ids)
-    fetch_raw.start()
+    for q in range(4):
+        fetch_raw(q).start()
     fetch_ids.start()
     barrier = pltpu.get_barrier_semaphore()
 
@@ -80,79 +84,6 @@
 
     for other in (sib, up, down):
         pl.semaphore_signal(barrier, inc=1, device_id=(other, me), device_id_type=MESH)
-    fetch_raw.wait()
-    own[...] = raw[...].reshape(GROUPS, GROUP, F).astype(jnp.bfloat16)
-    pl.semaphore_wait(barrier, TEAM + 2)
-
-    def relay_of(wave, row, side):
-        return 4 * row + 2 * side + lax.rem(row + wave + core, 2)
-
-    my_x, my_y = lax.rem(me, 4), me // 4
-    my_group = 4 * lax.rem(my_x + my_y + core, 2) + my_y
-    my_side = my_x // 2
-
-    def piece(side):
-        return pl.ds(*SPLIT[side])
-
-    def copy1(wave, row, side):
-        g = 4 * wave + row
-        return pltpu.make_async_remote_copy(
-            src_ref=own.at[g, :, piece(side)],
-            dst_ref=mid.at[me, :, piece(side)],
-            send_sem=send1.at[2 * g + side],
-            recv_sem=recv1.at[me],
-            device_id=(dp, relay_of(wave, row, side)),
-            device_id_type=MESH,
-        )
-
-    def arrive1(s, side):
-        return pltpu.make_async_remote_copy(
-            src_ref=own.at[0, :, piece(side)],
-            dst_ref=mid.at[s, :, piece(side)],
-            send_sem=send1.at[0],
-            recv_sem=recv1.at[s],
-            device_id=(dp, s),
-            device_id_type=MESH,
-        )
-
-    def copy2(e, side):
-        return pltpu.make_async_remote_copy(
-            src_ref=stage.at[e, :, piece(side)],
-            dst_ref=slots.at[0, my_group, :, piece(side)],
-            send_sem=send2.at[e],
-            recv_sem=recv2.at[2 * my_group + side],
-            device_id=(dp, e),
-            device_id_type=MESH,
-        )
-
-    def arrive2(wave, row, side):
-        g = 4 * wave + row
-        return pltpu.make_async_remote_copy(
-            src_ref=stage.at[0, :, piece(side)],
-            dst_ref=slots.at[0, g, :, piece(side)],
-            send_sem=send2.at[0],
-            recv_sem=recv2.at[2 * g + side],
-            device_id=(dp, relay_of(wave, row, side)),
-            device_id_type=MESH,
-        )
-
-    for wave in range(2):
-
-        @pl.loop(0, 4)
-        def _(k):
-            row = lax.rem(k + me, 4)
-            for side in range(2):
-
-                @pl.when(relay_of(wave, row, side) != me)
-                def _():
-                    copy1(wave, row, side).start()
-
-    for side in range(2):
-
-        @pl.when(my_side == side)
-        def _():
-            mid[me, :, piece(side)] = own[my_group, :, piece(side)]
-
     fetch_ids.wait()
     values = [ids[j] for j in range(TEAM)]
     for e in range(TEAM):
@@ -161,6 +92,86 @@
             slot = jnp.where(values[j] == e, j, slot)
         holder[e] = slot
 
+    pl.semaphore_wait(barrier, TEAM + 2)
+
+    def swap(row):
+        return row // 2 + 2 * lax.rem(row, 2)
+
+    def relay_of(wave, row, side):
+        y = swap(row)
+        return 4 * y + 2 * side + lax.rem(y + wave + core, 2)
+
+    my_x, my_y = lax.rem(me, 4), me // 4
+    my_group = 4 * lax.rem(my_x + my_y + core, 2) + swap(my_y)
+    my_side = my_x // 2
+
+    def piece(side):
+        return pl.ds(*SPLIT[side])
+
+    def copy1(wave, row, side):
+        g = 4 * wave + row
+        return pltpu.make_async_remote_copy(
+            src_ref=own.at[g, :, piece(side)],
+            dst_ref=mid.at[me, :, piece(side)],
+            send_sem=send1.at[2 * g + side],
+            recv_sem=recv1.at[me],
+            device_id=(dp, relay_of(wave, row, side)),
+            device_id_type=MESH,
+        )
+
+    def arrive1(s, side):
+        return pltpu.make_async_remote_copy(
+            src_ref=own.at[0, :, piece(side)],
+            dst_ref=mid.at[s, :, piece(side)],
+            send_sem=send1.at[0],
+            recv_sem=recv1.at[s],
+            device_id=(dp, s),
+            device_id_type=MESH,
+        )
+
+    def copy2(e, side):
+        return pltpu.make_async_remote_copy(
+            src_ref=stage.at[e, :, piece(side)],
+            dst_ref=slots.at[0, my_group, :, piece(side)],
+            send_sem=send2.at[e],
+            recv_sem=recv2.at[2 * my_group + side],
+            device_id=(dp, e),
+            device_id_type=MESH,
+        )
+
+    def arrive2(wave, row, side):
+        g = 4 * wave + row
+        return pltpu.make_async_remote_copy(
+            src_ref=stage.at[0, :, piece(side)],
+            dst_ref=slots.at[0, g, :, piece(side)],
+            send_sem=send2.at[0],
+            recv_sem=recv2.at[2 * g + side],
+            device_id=(dp, relay_of(wave, row, side)),
+            device_id_type=MESH,
+        )
+
+    for q in range(4):
+        fetch_raw(q).wait()
+        own[2 * q : 2 * q + 2] = (
+            raw[32 * q : 32 * q + 32].reshape(2, GROUP, F).astype(jnp.bfloat16)
+        )
+        wave = q // 2
+
+        @pl.loop(0, 2)
+        def _(k):
+            row = 2 * (q % 2) + lax.rem(k + me, 2)
+            for side in range(2):
+
+                @pl.when(relay_of(wave, row, side) != me)
+                def _():
+                    copy1(wave, row, side).start()
+
+    for side in range(2):
+
+        @pl.when(my_side == side)
+        def _():
+            mid[me, :, piece(side)] = own[my_group, :, piece(side)]
+
     for side in range(2):
 
         @pl.when(my_side == side)
@@ -183,25 +194,22 @@
     def part(first_group, count):
         return pl.ds(first_group, count)
 
-    half = GROUPS // 2
-    lower, upper = part(0, half), part(half, half)
-
-    def copy_up(src, src_part, t, dst_part, sem):
-        return pltpu.make_async_remote_copy(
-            src_ref=slots.at[src, src_part],
-            dst_ref=slots.at[t, dst_part],
-            send_sem=send_up.at[sem],
-            recv_sem=recv_up.at[sem],
+    def up_piece(src, first_group, t, p):
+        return pltpu.make_async_remote_copy(
+            src_ref=slots.at[src, part(first_group + 2 * p, 2)],
+            dst_ref=slots.at[t, part(2 * p, 2)],
+            send_sem=send_up.at[2 * t + p],
+            recv_sem=recv_up.at[2 * t + p],
             device_id=(up, me),
             device_id_type=MESH,
         )
 
-    def copy_down(src, src_part, t, dst_part, sem):
-        return pltpu.make_async_remote_copy(
-            src_ref=slots.at[src, src_part],
-            dst_ref=slots.at[t, dst_part],
-            send_sem=send_down.at[sem],
-            recv_sem=recv_down.at[sem],
+    def down_piece(src, first_group, t, p):
+        return pltpu.make_async_remote_copy(
+            src_ref=slots.at[src, part(first_group + 2 * p, 2)],
+            dst_ref=slots.at[t, part(4 + 2 * p, 2)],
+            send_sem=send_down.at[2 * t + p],
+            recv_sem=recv_down.at[2 * t + p],
             device_id=(down, me),
             device_id_type=MESH,
         )
@@ -216,27 +224,20 @@
             device_id_type=MESH,
         )
 
-    def down_piece(src, t, p):
-        rows = part(half + 2 * p, 2)
-        return copy_down(src, rows, t, rows, STEPS - 2 + 2 * (t - (STEPS - 2)) + p)
-
     for wave in range(2):
-
-        @pl.loop(0, 4)
-        def _(row):
-            for side in range(2):
-
-                @pl.when(relay_of(wave, row, side) != me)
-                def _():
-                    arrive2(wave, row, side).wait_recv()
-
-        if wave == 1:
-            copy_sib(0).start()
-            copy_up(0, lower, 1, lower, 1).wait_send()
-            copy_down(0, lower, 1, upper, 1).wait_send()
-        sent = part(4 * wave, 4)
-        copy_up(0, sent, wave + 1, lower, wave + 1).start()
-        copy_down(0, sent, wave + 1, upper, wave + 1).start()
+        for p in range(2):
+
+            @pl.loop(2 * p, 2 * p + 2)
+            def _(row):
+                for side in range(2):
+
+                    @pl.when(relay_of(wave, row, side) != me)
+                    def _():
+                        arrive2(wave, row, side).wait_recv()
+
+            up_piece(0, 4 * wave, wave + 1, p).start()
+            down_piece(0, 4 * wave, wave + 1, p).start()
+    copy_sib(0).start()
 
     def turn(t, side):
         turned[:, side * ROWS : (side + 1) * ROWS] = (
@@ -265,28 +266,24 @@
     def _(k):
         t = k + 1
 
-        @pl.when(t == STEPS - 2)
+        @pl.when(t < STEPS - 1)
         def _():
             for p in range(2):
-                down_piece(4, 6, p).wait_recv()
-                down_piece(6, 7, p).start()
-            copy_up(4, lower, 6, lower, 6).wait_recv()
-            copy_sib(t).start()
-
-        @pl.when(t < STEPS - 2)
-        def _():
-            copy_up(t, lower, t, lower, t).wait_recv()
-            copy_up(t, lower, t + 2, lower, t + 2).start()
-            copy_down(t, upper, t, upper, t).wait_recv()
-
-            @pl.when(t < STEPS - 4)
-            def _():
-                copy_down(t, upper, t + 2, upper, t + 2).start()
-
-            @pl.when(t == STEPS - 4)
-            def _():
-                for p in range(2):
-                    down_piece(4, 6, p).start()
+                up_piece(t, 0, t, p).wait_recv()
+
+                @pl.when(t < STEPS - 2)
+                def _():
+                    up_piece(t, 0, t + 2, p).start()
+
+                down_piece(t, 4, t, p).wait_recv()
+
+                @pl.when(t < STEPS - 3)
+                def _():
+                    down_piece(t, 4, t + 2, p).start()
+
+                @pl.when(t == STEPS - 2)
+                def _():
+                    down_piece(t, 4, t + 1, p).start()
 
             copy_sib(t).start()
 
@@ -316,25 +313,20 @@
             def _(k):
                 copy2(lax.rem(me + k, TEAM), side).wait_send()
 
-    @pl.loop(2, STEPS - 1)
+    @pl.loop(1, STEPS - 1)
     def _(t):
-        copy_up(t, lower, t, lower, t).wait_send()
-
-        @pl.when(t < STEPS - 2)
-        def _():
-            copy_down(t, upper, t, upper, t).wait_send()
+        for p in range(2):
+            up_piece(t, 0, t, p).wait_send()
+            down_piece(t, 4, t, p).wait_send()
 
     @pl.loop(0, STEPS - 1)
     def _(t):
         copy_sib(t).wait_send()
 
+    last = STEPS - 1
     for p in range(2):
-        down_piece(4, 6, p).wait_send()
-
-    last = STEPS - 1
-    copy_up(5, lower, last, lower, last).wait_recv()
-    for p in range(2):
-        down_piece(6, last, p).wait_recv()
+        up_piece(last, 0, last, p).wait_recv()
+        down_piece(last, 4, last, p).wait_recv()
     copy_sib(last).start()
     meet(last)
     apply(last)
@@ -410,9 +402,9 @@
     product(right, keep(left))
     poly(left, right, third)
 
-    down_piece(6, last, 0).wait_send()
-    down_piece(6, last, 1).wait_send()
-    copy_up(5, lower, last, lower, last).wait_send()
+    for p in range(2):
+        up_piece(last, 0, last, p).wait_send()
+        down_piece(last, 4, last, p).wait_send()
     copy_sib(last).wait_send()
 
 
@@ -439,16 +431,16 @@
             pltpu.VMEM((ROWS, F), f32),
             pltpu.VMEM((ROWS, F), bf16),
             pltpu.VMEM((ROWS, F), bf16),
-            dma,
+            dma((4,)),
             dma,
             dma((2 * GROUPS,)),
             dma((TEAM,)),
             dma((TEAM,)),
             dma((2 * GROUPS,)),
-            dma((STEPS,)),
-            dma((STEPS,)),
-            dma((STEPS + 2,)),
-            dma((STEPS + 2,)),
+            dma((2 * STEPS,)),
+            dma((2 * STEPS,)),
+            dma((2 * STEPS,)),
+            dma((2 * STEPS,)),
             dma((STEPS,)),
             dma((STEPS,)),
         ],

time: 64.5 us -> 63.9 us (level)
  no operation moved by 1% of the time
where the time goes in v8:
time: 63.9 us; the launch traced here: 63.8 us
  Pallas kernels  62.4 us (98%)
  local copies, waits for them, and re-layouts  1.39 us (2%)
    pallas_call x1, Pallas kernels, body(): pl.pallas_call(kernel, out_shape=jax.ShapeDtypeStruct((ROWS, F), bf16), i...  62.4 us
    unnamed x3, local copies, waits for them, and re-layouts  1.39 us

profile of v8, /device:TPU:1, one launch (start us, length us, event | category | flops | bytes accessed | tf_op | source)
XLA Modules:
  0.0 63.8 jit_solution(14681726867701087506)
XLA Ops:
  0.0 0.0 copy-start
  0.0 0.7 %copy-done = s32[16]{0:T(128)S(1)} copy-done((s32[16]{0:T(128)S(1)}, s32[16]{0:T(128)}, u32[]{:S(2)}) %copy-start) | copy-done | bytes 88
  0.7 62.4 %shard_map.28 = bf16[128,1408]{1,0:T(8,128)(2,1)S(1)} custom-call(f32[128,1408]{1,0:T(8,128)} %bitcast.3, s32[16]{0:T(128)S(1)} %copy-done), custom_call_target="tpu_custom_call" | custom-call | flops 14210301952 | bytes 1081344 | tf_op jit(solution)/shard_map/pallas_call | solution.py:414
  63.1 0.7 %copy.4 = bf16[1,128,1408]{2,1,0:T(8,128)(2,1)} copy(bf16[1,128,1408]{2,1,0:T(8,128)(2,1)S(1)} %bitcast.2) | data formatting | bytes 720896
Async XLA Ops:
  0.0 0.7 %copy-start = (s32[16]{0:T(128)S(1)}, s32[16]{0:T(128)}, u32[]{:S(2)}) copy-start(s32[16]{0:T(128)} %ids_ref.1) | copy-start | bytes 196

commit v9 on v8

--- a/solution.py
+++ b/solution.py
@@ -185,9 +185,13 @@
             for e in range(TEAM):
                 stage[e, :, piece(side)] = mid[holder[e], :, piece(side)]
 
-            @pl.loop(1, TEAM)
+            @pl.loop(0, TEAM)
             def _(k):
-                copy2(lax.rem(me + k, TEAM), side).start()
+                e = jnp.where(k == 0, 0, 1 + lax.rem(me + k, TEAM - 1))
+
+                @pl.when(e != me)
+                def _():
+                    copy2(e, side).start()
 
             slots[0, my_group, :, piece(side)] = stage[me, :, piece(side)]
 

time: 63.9 us -> 63.6 us (level)
  no operation moved by 1% of the time
where the time goes in v9:
time: 63.6 us; the launch traced here: 63.5 us
  Pallas kernels  62.1 us (98%)
  local copies, waits for them, and re-layouts  1.39 us (2%)
    pallas_call x1, Pallas kernels, body(): pl.pallas_call(kernel, out_shape=jax.ShapeDtypeStruct((ROWS, F), bf16), i...  62.1 us
    unnamed x3, local copies, waits for them, and re-layouts  1.39 us

profile of v9, /device:TPU:1, one launch (start us, length us, event | category | flops | bytes accessed | tf_op | source)
XLA Modules:
  0.0 63.5 jit_solution(1495642122113293441)
XLA Ops:
  0.0 0.0 copy-start
  0.0 0.7 %copy-done = s32[16]{0:T(128)S(1)} copy-done((s32[16]{0:T(128)S(1)}, s32[16]{0:T(128)}, u32[]{:S(2)}) %copy-start) | copy-done | bytes 88
  0.7 62.1 %shard_map.28 = bf16[128,1408]{1,0:T(8,128)(2,1)S(1)} custom-call(f32[128,1408]{1,0:T(8,128)} %bitcast.3, s32[16]{0:T(128)S(1)} %copy-done), custom_call_target="tpu_custom_call" | custom-call | flops 14210301952 | bytes 1081344 | tf_op jit(solution)/shard_map/pallas_call | solution.py:418
  62.8 0.7 %copy.4 = bf16[1,128,1408]{2,1,0:T(8,128)(2,1)} copy(bf16[1,128,1408]{2,1,0:T(8,128)(2,1)S(1)} %bitcast.2) | data formatting | bytes 720896
Async XLA Ops:
  0.0 0.7 %copy-start = (s32[16]{0:T(128)S(1)}, s32[16]{0:T(128)}, u32[]{:S(2)}) copy-start(s32[16]{0:T(128)} %ids_ref.1) | copy-start | bytes 196

commit v10 on v8

--- a/solution.py
+++ b/solution.py
@@ -253,14 +253,8 @@
         turn(t, 1)
 
     gram[...] = jnp.zeros_like(gram)
-    base[...] = jnp.zeros_like(base)
     left[...] = slots[0, 0:GROUPS].reshape(ROWS, F)
-
-    def apply(t):
-        inner = jnp.dot(left[...], turned[...], preferred_element_type=jnp.float32)
-        base[...] += jnp.dot(
-            inner.astype(jnp.bfloat16), columns(t, 0, F), preferred_element_type=jnp.float32
-        )
+    base[...] = left[...].astype(jnp.float32)
 
     @pl.loop(0, STEPS - 1)
     def _(k):
@@ -293,7 +287,6 @@
             gram[0:end, start:end] += jnp.dot(
                 turned[0:end, :], columns(k, start, size), preferred_element_type=jnp.float32
             )
-        apply(k)
 
     for wave in range(2):
 
@@ -329,7 +322,6 @@
         down_piece(last, 4, last, p).wait_recv()
     copy_sib(last).start()
     meet(last)
-    apply(last)
     squares = jnp.zeros((8, 128), jnp.float32)
     for start, size in PANELS:
         end = start + size
@@ -393,8 +385,7 @@
         result = total[:, cols] + coef_c * value
         out_ref[:, cols] = (math.sqrt(max(D, F)) * result).astype(jnp.bfloat16)
 
-    linear(slice(0, F), left[...].astype(jnp.float32), inverse * base[...], right)
-    quadratic(right, first)
+    poly(left, right, first)
     poly(left, right, keep(left))
     product(left, keep(right))
     poly(right, left, second)

time: 63.9 us -> 63.4 us (level)
  no operation moved by 1% of the time
where the time goes in v10:
time: 63.4 us; the launch traced here: 63.3 us
  Pallas kernels  61.9 us (98%)
  local copies, waits for them, and re-layouts  1.39 us (2%)
    pallas_call x1, Pallas kernels, body(): pl.pallas_call(kernel, out_shape=jax.ShapeDtypeStruct((ROWS, F), bf16), i...  61.9 us
    unnamed x3, local copies, waits for them, and re-layouts  1.39 us

profile of v10, /device:TPU:1, one launch (start us, length us, event | category | flops | bytes accessed | tf_op | source)
XLA Modules:
  0.0 63.3 jit_solution(14421708842184715579)
XLA Ops:
  0.0 0.0 copy-start
  0.0 0.7 %copy-done = s32[16]{0:T(128)S(1)} copy-done((s32[16]{0:T(128)S(1)}, s32[16]{0:T(128)}, u32[]{:S(2)}) %copy-start) | copy-done | bytes 88
  0.7 61.9 %shard_map.28 = bf16[128,1408]{1,0:T(8,128)(2,1)S(1)} custom-call(f32[128,1408]{1,0:T(8,128)} %bitcast.3, s32[16]{0:T(128)S(1)} %copy-done), custom_call_target="tpu_custom_call" | custom-call | flops 14210301952 | bytes 1081344 | tf_op jit(solution)/shard_map/pallas_call | solution.py:405
  62.6 0.7 %copy.4 = bf16[1,128,1408]{2,1,0:T(8,128)(2,1)} copy(bf16[1,128,1408]{2,1,0:T(8,128)(2,1)S(1)} %bitcast.2) | data formatting | bytes 720896
Async XLA Ops:
  0.0 0.7 %copy-start = (s32[16]{0:T(128)S(1)}, s32[16]{0:T(128)}, u32[]{:S(2)}) copy-start(s32[16]{0:T(128)} %ids_ref.1) | copy-start | bytes 196
